TPU v7x, 512 devices: a whole 4x4x16 slice. The times are simulated.
512 devices in a mesh: grp: 8 (over x, core), vocab: 64 (over y, z).
Axes of the slice: x: 4, y: 4, z: 16, core: 2. Of those that a mesh axis runs over, the one named last changes fastest.
Arguments:
- student_hidden: bfloat16 [1024, 5120], P(('grp', 'vocab')), parts along dimension 0, may hold values from -64 to 64
- teacher_hidden: bfloat16 [1024, 4096], P(('grp', 'vocab')), parts along dimension 0, may hold values from -64 to 64
- student_head: bfloat16 [81920, 5120], P('vocab'), may hold values from -1 to 1
- teacher_head: bfloat16 [81920, 4096], P('vocab'), may hold values from -1 to 1
- row_weight: float32 [1024], P(('grp', 'vocab')), parts along dimension 0, may hold values from 64 to 512
Outputs:
- hidden_grad: bfloat16 [1024, 5120], P(('grp', 'vocab')), parts along dimension 0
There are 8 independent parts, one for each index of `grp`. A program takes and returns all parts, laid end to end along the dimension named above; an argument that names none is the same for every part. Nothing has to cross between parts.
All inputs are finite; a program needn't handle non-finite values.
Results may differ from a plain program's by a relative error of at most 0.0043.
Values may be sent and summed in bfloat16 or wider, within the bound.
No kernel may reach another device: no remote copies, remote signals or barrier semaphores. Data moves between devices by JAX's collectives and lax.ppermute only.
A program may use at most 128 MiB of HBM per device.

v0:
```python
import jax
import jax.numpy as jnp
from jax import lax
from jax.sharding import PartitionSpec as P


def local(student_hidden, teacher_hidden, student_head, teacher_head, row_weight):
    student_logits = lax.dot_general(
        lax.all_gather(student_hidden, "vocab", axis=0, tiled=True),
        student_head,
        (((1,), (1,)), ((), ())),
        preferred_element_type=jnp.float32,
    )
    teacher_logits = lax.dot_general(
        lax.all_gather(teacher_hidden, "vocab", axis=0, tiled=True),
        teacher_head,
        (((1,), (1,)), ((), ())),
        preferred_element_type=jnp.float32,
    )
    student_top, teacher_top = lax.pmax(
        (jnp.max(student_logits, axis=1), jnp.max(teacher_logits, axis=1)), "vocab"
    )
    student_exp = jnp.exp(student_logits - student_top[:, None])
    teacher_exp = jnp.exp(teacher_logits - teacher_top[:, None])
    student_total, teacher_total = lax.psum(
        (jnp.sum(student_exp, axis=1), jnp.sum(teacher_exp, axis=1)), "vocab"
    )
    difference = (
        student_exp / student_total[:, None] - teacher_exp / teacher_total[:, None]
    ).astype(jnp.bfloat16)
    summed = lax.psum_scatter(
        jnp.dot(difference, student_head, preferred_element_type=jnp.float32),
        "vocab",
        scatter_dimension=0,
        tiled=True,
    )
    return (row_weight[:, None] * summed).astype(jnp.bfloat16)


def solution(mesh):
    in_specs = (
        P(("grp", "vocab"), None),
        P(("grp", "vocab"), None),
        P("vocab", None),
        P("vocab", None),
        P(("grp", "vocab")),
    )
    out_specs = P(("grp", "vocab"), None)
    return jax.shard_map(local, mesh=mesh, in_specs=in_specs, out_specs=out_specs, check_vma=False)
```

profile of v0, /device:TPU:6, one launch (start us, length us, event | category | flops | bytes accessed | tf_op | source)
XLA Modules:
  0.0 873.0 jit_solution(13701660763919657645)
XLA Ops:
  6.5 0.0 all-gather.7.cloned.1.call-start
  6.5 0.7 all-gather.7.cloned.1.call-update
  7.3 0.0 all-gather.5.cloned.1.call-start
  7.3 0.7 all-gather.5.cloned.1.call-update
  8.0 0.0 all-reduce.5.cloned.1.call-start
  8.1 145.7 %all-gather.7.cloned.1.call-done = bf16[64,2,4096]{2,1,0:T(2,128)(2,1)} async-done(((bf16[1,2,4096]{2,1,0:T(2,128)(2,1)}), bf16[64,2,4096]{2,1,0:T(2,128)(2,1)}) %all-gather.7.cloned.1.call-update) | async-done | bytes 1048592 | tf_op jit(solution)/shard_map/all_gather | solution.py:15
  153.7 1.5 reshape.8
  155.2 7.6 fusion.8
  162.8 129.8 %all-gather.5.cloned.1.call-done = bf16[64,2,5120]{2,1,0:T(2,128)(2,1)} async-done(((bf16[1,2,5120]{2,1,0:T(2,128)(2,1)}), bf16[64,2,5120]{2,1,0:T(2,128)(2,1)}) %all-gather.5.cloned.1.call-update) | async-done | bytes 1310736 | tf_op jit(solution)/shard_map/all_gather | solution.py:9
  292.6 3.1 reshape.6
  295.7 9.2 %fusion.9 = (f32[128]{0:T(128)S(1)}, f32[128,1280]{1,0:T(8,128)S(1)}) fusion(bf16[128,5120]{1,0:T(8,128)(2,1)S(1)} %reshape.6, bf16[1280,5120]{1,0:T(8,128)(2,1)} %param.7), kind=kOutput, calls=%fused_computation.13 | convolution fusion | flops 1677885312 | bytes 15073792 | tf_op jit(solution)/shard_map/dot_general | solution.py:8
  304.9 141.4 %all-reduce.2 = (f32[128]{0:T(128)S(1)}, f32[128]{0:T(128)S(1)}) all-reduce(f32[128]{0:T(128)S(1)} %get-tuple-element.9, f32[128]{0:T(128)S(1)} %get-tuple-element.11), channel_id=1, replica_groups=mesh['grp'=8,'vocab'=64] {'vocab'}, use_global_device_ids=true, to_apply=%region_5.0 | all-reduce | flops 256 | bytes 2048 | tf_op jit(solution)/shard_map/pmax | solution.py:20
  446.3 0.3 fusion
  446.7 138.0 %all-reduce.1 = (f32[128]{0:T(128)S(1)}, f32[128]{0:T(128)S(1)}) all-reduce(f32[128]{0:T(128)S(1)} %get-tuple-element.14, f32[128]{0:T(128)S(1)} %get-tuple-element.13), channel_id=1, replica_groups=mesh['grp'=8,'vocab'=64] {'vocab'}, use_global_device_ids=true, to_apply=%region_7.0 | all-reduce | flops 256 | bytes 2048 | tf_op jit(solution)/shard_map/psum | solution.py:25
  584.6 0.0 copy-start
  584.6 8.3 fusion.2
  593.0 0.0 all-reduce.5.cloned.1.call-update
  593.0 1.3 dynamic-slice
  594.9 269.9 %all-reduce.5.cloned.1.call-done = f32[128,5120]{1,0:T(8,128)} async-done(((f32[128,5120]{1,0:T(8,128)}), f32[128,5120]{1,0:T(8,128)}) %all-reduce.5.cloned.1.call-update) | async-done | bytes 2621456
  864.9 0.0 copy-done
  864.9 1.6 fusion.7
Async XLA Ops:
  6.5 147.2 %all-gather.7.cloned.1.call-start = ((), (), s32[]{:S(2)}) async-start(), calls=%async_computation.1 | async-start | bytes 1064960 | tf_op jit(solution)/shard_map/all_gather | solution.py:15
  7.3 285.3 %all-gather.5.cloned.1.call-start = ((), (), s32[]{:S(2)}) async-start(), calls=%async_computation | async-start | bytes 1331200 | tf_op jit(solution)/shard_map/all_gather | solution.py:9
  8.0 856.8 %all-reduce.5.cloned.1.call-start = ((), (), s32[]{:S(2)}) async-start(), calls=%async_computation.2 | async-start | bytes 5242880
  584.6 280.2 %copy-start = (f32[2]{0:T(128)S(1)}, f32[2]{0:T(128)}, u32[]{:S(2)}) copy-start(f32[2]{0:T(128)} %param.9) | copy-start | bytes 28
Sparse Core Ops, SparseCore 0:
  10.3 143.3 all-gather.6
  156.7 135.8 all-gather.4
  593.1 271.6 all-reduce.4
where the time goes:
time: 873 us
  waiting for transfers between devices  547 us (63%)
  blocking collectives  279 us (32%)
  matrix products  25.2 us (3%)
  between operations  13.8 us (2%)
    unnamed x4, waiting for transfers between devices  271 us
    all_gather x1, waiting for transfers between devices, local(): lax.all_gather(teacher_hidden, 'vocab', axis=0, tiled=True)  146 us
    pmax x1, blocking collectives, local(): lax.pmax((jnp.max(student_logits, axis=1), jnp.max(teacher_logits, axis=1...  141 us
    psum x1, blocking collectives, local(): lax.psum((jnp.sum(student_exp, axis=1), jnp.sum(teacher_exp, axis=1)), 'v...  138 us
    all_gather x1, waiting for transfers between devices, local(): lax.all_gather(student_hidden, 'vocab', axis=0, tiled=True)  130 us
  transfers between devices with their start and end apart: 3, of which 3 were waited for; matrix products, arithmetic and copies ran while one was open for 1% of the time, Pallas kernels for 0%

commit v1 on v0

v1 whole, which is shorter than its diff:
```python
import jax
import jax.numpy as jnp
from jax import lax
from jax.sharding import Mesh, PartitionSpec as P

Y, Z = 4, 16
DIMS = (((1,), (1,)), ((), ()))


def to_all(x, axis, size):
    return lax.all_to_all(jnp.broadcast_to(x[None], (size, *x.shape)), axis, 0, 0)


def local(student_hidden, teacher_hidden, student_head, teacher_head, row_weight):
    ds, dt = student_hidden.shape[1], teacher_hidden.shape[1]
    mine = jnp.concatenate([student_hidden, teacher_hidden], axis=1)
    plane = to_all(mine, "z", Z).reshape(Z * 2, ds + dt)
    student_rows = to_all(plane[:, :ds], "y", Y).reshape(Y * Z * 2, ds)
    teacher_rows = to_all(plane[:, ds:], "y", Y).reshape(Y * Z * 2, dt)
    student_logits = lax.dot_general(student_rows, student_head, DIMS, preferred_element_type=jnp.float32)
    teacher_logits = lax.dot_general(teacher_rows, teacher_head, DIMS, preferred_element_type=jnp.float32)
    student_top = jnp.max(student_logits, axis=1)
    teacher_top = jnp.max(teacher_logits, axis=1)
    student_exp = jnp.exp(student_logits - student_top[:, None])
    teacher_exp = jnp.exp(teacher_logits - teacher_top[:, None])
    stats = jnp.stack(
        [student_top, teacher_top, jnp.sum(student_exp, axis=1), jnp.sum(teacher_exp, axis=1)]
    )
    every = to_all(stats, ("y", "z"), Y * Z)
    tops = jnp.max(every[:, :2], axis=0)
    totals = jnp.sum(every[:, 2:] * jnp.exp(every[:, :2] - tops), axis=0)
    factors = jnp.exp(stats[:2] - tops) / totals
    difference = (student_exp * factors[0][:, None] - teacher_exp * factors[1][:, None]).astype(jnp.bfloat16)
    partial = jnp.dot(difference, student_head, preferred_element_type=jnp.float32).astype(jnp.bfloat16)
    over_y = lax.all_to_all(partial.reshape(Y, Z * 2, ds), "y", 0, 0)
    over_y = jnp.sum(over_y.astype(jnp.float32), axis=0).astype(jnp.bfloat16)
    over_z = lax.all_to_all(over_y.reshape(Z, 2, ds), "z", 0, 0)
    summed = jnp.sum(over_z.astype(jnp.float32), axis=0)
    return (row_weight[:, None] * summed).astype(jnp.bfloat16)


def solution(mesh):
    split = Mesh(mesh.devices.reshape(-1, Y, Z), ("grp", "y", "z"))
    rows = P(("grp", "y", "z"))
    head = P(("y", "z"))
    return jax.shard_map(
        local, mesh=split, in_specs=(rows, rows, head, head, rows), out_specs=rows, check_vma=False
    )
```

time: 873 us -> 169 us (0.19)
  waiting for transfers between devices: 547 us -> 17.9 us
  blocking collectives: 279 us -> 113 us
  between operations: 13.8 us -> 0.09 us
    all_gather x2 -> x0, waiting for transfers between devices: 275 us -> none  [the longest x1 146 us: local(): lax.all_gather(teacher_hidden, 'vocab', axis=0, tiled=True)]
    unnamed x4 -> x0, waiting for transfers between devices: 271 us -> none
    pmax x1 -> x0, blocking collectives: 141 us -> none  [local(): lax.pmax((jnp.max(student_logits, axis=1), jnp.max(teacher_logits, axis=1...]
    psum x1 -> x0, blocking collectives: 138 us -> none  [local(): lax.psum((jnp.sum(student_exp, axis=1), jnp.sum(teacher_exp, axis=1)), 'v...]
    all_to_all x0 -> x4, blocking collectives: none -> 113 us  [the longest x2 75.4 us: to_all(): lax.all_to_all(jnp.broadcast_to(x[None], (size, *x.shape)), axis, 0, 0)]
    all_to_all x0 -> x2, waiting for transfers between devices: none -> 17.9 us  [to_all(): lax.all_to_all(jnp.broadcast_to(x[None], (size, *x.shape)), axis, 0, 0)]
  transfers between devices with their start and end apart: 3 -> 2, of which waited for: 3 -> 2; matrix products, arithmetic and copies ran while one was open for 1% -> 5% of each run, Pallas kernels for 0% -> 0%
where the time goes in v1:
time: 169 us; the launch traced here: 168 us
  blocking collectives  113 us (67%)
  matrix products  23.6 us (14%)
  waiting for transfers between devices  17.9 us (11%)
  starting transfers between devices  8 us (5%)
  local copies, waits for them, and re-layouts  3.02 us (2%)
  other arithmetic  2.62 us (2%)
    all_to_all x2, blocking collectives, to_all(): lax.all_to_all(jnp.broadcast_to(x[None], (size, *x.shape)), axis, 0, 0)  75.4 us
    all_to_all x1, blocking collectives, local(): over_z = lax.all_to_all(over_y.reshape(Z, 2, ds), 'z', 0, 0)  20.2 us
    all_to_all x2, waiting for transfers between devices, to_all(): lax.all_to_all(jnp.broadcast_to(x[None], (size, *x.shape)), axis, 0, 0)  17.9 us
    all_to_all x1, blocking collectives, local(): over_y = lax.all_to_all(partial.reshape(Y, Z * 2, ds), 'y', 0, 0)  17.4 us
    dot_general x1, matrix products, local(): lax.dot_general(student_rows, student_head, DIMS, preferred_element_type=...  9.21 us
    all_to_all x2, starting transfers between devices, to_all(): lax.all_to_all(jnp.broadcast_to(x[None], (size, *x.shape)), axis, 0, 0)  8 us
    dot_general x1, matrix products, local(): lax.dot_general(teacher_rows, teacher_head, DIMS, preferred_element_type=...  7.65 us
    dot_general x1, matrix products, local(): jnp.dot(difference, student_head, preferred_element_type=jnp.float32)  6.74 us
  transfers between devices with their start and end apart: 2, of which 2 were waited for; matrix products, arithmetic and copies ran while one was open for 5% of the time, Pallas kernels for 0%

profile of v1, /device:TPU:6, one launch (start us, length us, event | category | flops | bytes accessed | tf_op | source)
XLA Modules:
  0.0 168.3 jit_solution(7900533529414742288)
XLA Ops:
  0.0 0.8 pad_maximum_fusion
  0.8 0.3 broadcast_in_dim.8
  1.1 49.9 %all_to_all.30 = bf16[16,2,9216]{2,1,0:T(2,128)(2,1)S(1)} all-to-all(bf16[16,2,9216]{2,1,0:T(2,128)(2,1)S(1)} %broadcast_in_dim.8), channel_id=1, replica_groups=mesh['grp'=8,'y'=4,'z'=16] {'z'}, dimensions={0} | all-to-all | bytes 1179648 | tf_op jit(solution)/shard_map/all_to_all | solution.py:11
  51.0 0.2 reshape.25
  51.3 1.1 broadcast_in_dim.10
  52.4 4.5 %all-to-all-start.2 = ((bf16[4,32,4096]{2,1,0:T(8,128)(2,1)}), bf16[4,32,4096]{2,1,0:T(8,128)(2,1)S(1)}, u32[]{:S(2)}, u32[]{:S(2)}) async-start(bf16[4,32,4096]{2,1,0:T(8,128)(2,1)} %broadcast_in_dim.10), calls=%async_computation.2 | async-start | bytes 2097152 | tf_op jit(solution)/shard_map/all_to_all | solution.py:11
  56.9 12.1 %all-to-all-done.2 = bf16[4,32,4096]{2,1,0:T(8,128)(2,1)S(1)} async-done(((bf16[4,32,4096]{2,1,0:T(8,128)(2,1)}), bf16[4,32,4096]{2,1,0:T(8,128)(2,1)S(1)}, u32[]{:S(2)}, u32[]{:S(2)}) %all-to-all-start.2) | async-done | bytes 1048608 | tf_op jit(solution)/shard_map/all_to_all | solution.py:11
  69.0 1.2 broadcast_in_dim.9
  70.2 3.5 %all-to-all-start.1 = ((bf16[4,32,5120]{2,1,0:T(8,128)(2,1)}), bf16[4,32,5120]{2,1,0:T(8,128)(2,1)S(1)}, u32[]{:S(2)}, u32[]{:S(2)}) async-start(bf16[4,32,5120]{2,1,0:T(8,128)(2,1)} %broadcast_in_dim.9), calls=%async_computation.1 | async-start | bytes 2621440 | tf_op jit(solution)/shard_map/all_to_all | solution.py:11
  73.7 7.6 %fusion.9 = (f32[128]{0:T(128)S(1)}, f32[128,1280]{1,0:T(8,128)S(1)}) fusion(bf16[128,4096]{1,0:T(8,128)(2,1)S(1)} %bitcast.18, bf16[1280,4096]{1,0:T(8,128)(2,1)} %param.8), kind=kOutput, calls=%fused_computation.22 | convolution fusion | flops 1342340992 | bytes 12190208 | tf_op jit(solution)/shard_map/dot_general | solution.py:21
  81.4 0.3 fusion.1
  81.6 5.8 %all-to-all-done.1 = bf16[4,32,5120]{2,1,0:T(8,128)(2,1)S(1)} async-done(((bf16[4,32,5120]{2,1,0:T(8,128)(2,1)}), bf16[4,32,5120]{2,1,0:T(8,128)(2,1)S(1)}, u32[]{:S(2)}, u32[]{:S(2)}) %all-to-all-start.1) | async-done | bytes 1310752 | tf_op jit(solution)/shard_map/all_to_all | solution.py:11
  87.4 9.2 %fusion.10 = (f32[128]{0:T(128)S(1)}, f32[128,1280]{1,0:T(8,128)S(1)}) fusion(bf16[128,5120]{1,0:T(8,128)(2,1)S(1)} %bitcast.16, bf16[1280,5120]{1,0:T(8,128)(2,1)} %param.7), kind=kOutput, calls=%fused_computation.23 | convolution fusion | flops 1677885312 | bytes 15073792 | tf_op jit(solution)/shard_map/dot_general | solution.py:20
  96.7 0.3 fusion
  97.0 25.5 %all_to_all.31 = f32[64,4,128]{2,1,0:T(4,128)S(1)} all-to-all(f32[64,4,128]{2,1,0:T(4,128)S(1)} %broadcast_in_dim.11), channel_id=1, replica_groups=mesh['grp'=8,'y'=4,'z'=16] {'y','z'}, dimensions={0} | all-to-all | bytes 262144 | tf_op jit(solution)/shard_map/all_to_all | solution.py:11
  122.5 0.1 slice_reduce_fusion
  122.5 0.1 fusion.6
  122.7 0.0 copy-start
  122.7 6.7 %convolution_convert_fusion = bf16[128,5120]{1,0:T(8,128)(2,1)S(1)} fusion(bf16[1280,5120]{1,0:T(8,128)(2,1)} %param.7, f32[128,1280]{1,0:T(8,128)S(1)} %get-tuple-element.10, f32[128,1280]{1,0:T(8,128)S(1)} %get-tuple-element.8, f32[128]{0:T(128)S(1)} %get-tuple-element.6, f32[128]{0:T(128)S(1)} %get-tuple-element.5, f32[128]{0:T(128)S(1)} %get-tuple-element.7, ...), kind=kOutput, calls=%fused_computation | convolution fusion | flops 1679360000 | bytes 15730688 | tf_op jit(solution)/shard_map/dot_general | solution.py:34
  129.4 17.4 %all_to_all.32 = bf16[4,32,5120]{2,1,0:T(8,128)(2,1)S(1)} all-to-all(bf16[4,32,5120]{2,1,0:T(8,128)(2,1)S(1)} %bitcast.17), channel_id=1, replica_groups=mesh['grp'=8,'y'=4,'z'=16] {'y'}, dimensions={0} | all-to-all | bytes 2621440 | tf_op jit(solution)/shard_map/all_to_all | solution.py:35
  146.8 0.3 reduce_sum.51
  147.1 0.1 reshape.29
  147.3 20.2 %all_to_all.33 = bf16[16,2,5120]{2,1,0:T(2,128)(2,1)S(1)} all-to-all(bf16[16,2,5120]{2,1,0:T(2,128)(2,1)S(1)} %reshape.29), channel_id=1, replica_groups=mesh['grp'=8,'y'=4,'z'=16] {'z'}, dimensions={0} | all-to-all | bytes 655360 | tf_op jit(solution)/shard_map/all_to_all | solution.py:37
  167.4 0.2 convert_reduce_fusion
  167.6 0.0 copy-done
  167.6 0.7 multiply_convert_fusion
  (6 shorter events, 0.1 us)
Async XLA Ops:
  52.4 16.6 %all-to-all-start.2 = ((bf16[4,32,4096]{2,1,0:T(8,128)(2,1)}), bf16[4,32,4096]{2,1,0:T(8,128)(2,1)S(1)}, u32[]{:S(2)}, u32[]{:S(2)}) async-start(bf16[4,32,4096]{2,1,0:T(8,128)(2,1)} %broadcast_in_dim.10), calls=%async_computation.2 | async-start | bytes 2097152 | tf_op jit(solution)/shard_map/all_to_all | solution.py:11
  70.2 17.3 %all-to-all-start.1 = ((bf16[4,32,5120]{2,1,0:T(8,128)(2,1)}), bf16[4,32,5120]{2,1,0:T(8,128)(2,1)S(1)}, u32[]{:S(2)}, u32[]{:S(2)}) async-start(bf16[4,32,5120]{2,1,0:T(8,128)(2,1)} %broadcast_in_dim.9), calls=%async_computation.1 | async-start | bytes 2621440 | tf_op jit(solution)/shard_map/all_to_all | solution.py:11
  122.7 44.9 %copy-start = (f32[2]{0:T(128)S(1)}, f32[2]{0:T(128)}, u32[]{:S(2)}) copy-start(f32[2]{0:T(128)} %param.9) | copy-start | bytes 28

commit v2 on v1

v2 whole, which is shorter than its diff:
```python
import jax
import jax.numpy as jnp
from jax import lax
from jax.experimental import pallas as pl
from jax.experimental.pallas import tpu as pltpu
from jax.sharding import Mesh, PartitionSpec as P

Y, Z, L = 4, 16, 2
H = Z // L
NEAR, FAR, ALL = ("y", "l"), "h", ("y", "h", "l")
DIMS = (((1,), (1,)), ((), ()))
MIB = 1 << 20
WIDE, DEEP = 512, 256
IN_VMEM = pl.BlockSpec(memory_space=pltpu.VMEM)
IN_HBM = pl.BlockSpec(memory_space=pltpu.HBM)


def to_all(x, axis, size):
    return lax.all_to_all(jnp.broadcast_to(x[None], (size, *x.shape)), axis, 0, 0)


def far_off(x):
    return pltpu.with_memory_space_constraint(x, pltpu.HBM)


def near(x):
    return pltpu.with_memory_space_constraint(x, pltpu.VMEM)


def spread_kernel(far_ref, out_ref):
    far = far_ref[...].astype(jnp.float32)
    block = jnp.concatenate([far[i] for i in range(far.shape[0])], axis=0).astype(out_ref.dtype)
    for i in range(out_ref.shape[0]):
        out_ref[i] = block


def spread(far):
    count, rows, width = far.shape
    return pl.pallas_call(
        spread_kernel,
        out_shape=jax.ShapeDtypeStruct((Y * L, count * rows, width), far.dtype),
        in_specs=[IN_VMEM],
        out_specs=IN_VMEM,
        compiler_params=pltpu.CompilerParams(vmem_limit_bytes=8 * MIB),
    )(far)


def fold_kernel(sums_ref, out_ref):
    total = jnp.sum(sums_ref[...].astype(jnp.float32), axis=0)
    for i in range(out_ref.shape[0]):
        out_ref[i] = total[2 * i : 2 * i + 2].astype(out_ref.dtype)


def fold(sums):
    width = sums.shape[2]
    return pl.pallas_call(
        fold_kernel,
        out_shape=jax.ShapeDtypeStruct((H, 2, width), sums.dtype),
        in_specs=[IN_VMEM],
        out_specs=IN_VMEM,
        compiler_params=pltpu.CompilerParams(vmem_limit_bytes=8 * MIB),
    )(sums)


def logits_kernel(
    rows_ref, student_far, teacher_far, student_exp, teacher_exp, stats_ref, student_near, teacher_near, sems
):
    rows = rows_ref.shape[0]
    pieces = student_far.shape[0] // DEEP
    heads = ((student_far, student_near, student_exp), (teacher_far, teacher_near, teacher_exp))

    def copy(k, i):
        part = pl.ds(i * DEEP, DEEP)
        return pltpu.make_async_copy(heads[k][0].at[part], heads[k][1].at[part], sems.at[k, i])

    for k in range(2):
        for i in range(pieces):
            copy(k, i).start()
    lane = lax.broadcasted_iota(jnp.int32, (rows, rows), 1)
    stats = jnp.zeros((rows, rows), jnp.float32)
    first = 0
    for k, (_, head, out) in enumerate(heads):
        width = head.shape[1]
        top = None
        for i in range(pieces):
            copy(k, i).wait()
            part = slice(i * DEEP, (i + 1) * DEEP)
            piece = lax.dot_general(
                rows_ref[:, first : first + width], head[part, :], DIMS, preferred_element_type=jnp.float32
            )
            out[:, part] = piece
            most = jnp.max(piece, axis=1, keepdims=True)
            top = most if top is None else jnp.maximum(top, most)
        exp = jnp.exp(out[...] - top)
        out[...] = exp
        total = jnp.sum(exp, axis=1, keepdims=True)
        stats = jnp.where(lane == k, top, jnp.where(lane == 2 + k, total, stats))
        first += width
    stats_ref[...] = jnp.transpose(stats)[:4]


def logits(every, student_head, teacher_head):
    rows, entries = every.shape[0], student_head.shape[0]
    return pl.pallas_call(
        logits_kernel,
        out_shape=(
            jax.ShapeDtypeStruct((rows, entries), jnp.float32),
            jax.ShapeDtypeStruct((rows, entries), jnp.float32),
            jax.ShapeDtypeStruct((4, rows), jnp.float32),
            pltpu.VMEM(student_head.shape, student_head.dtype),
        ),
        in_specs=[IN_VMEM, IN_HBM, IN_HBM],
        out_specs=[IN_VMEM] * 4,
        scratch_shapes=[
            pltpu.VMEM(teacher_head.shape, teacher_head.dtype),
            pltpu.SemaphoreType.DMA((2, entries // DEEP)),
        ],
        compiler_params=pltpu.CompilerParams(vmem_limit_bytes=24 * MIB),
    )(every, far_off(student_head), far_off(teacher_head))


def partial_kernel(student_exp, teacher_exp, stats_ref, all_ref, head, out, difference):
    rows = student_exp.shape[0]
    tops = jnp.max(all_ref[:, :2], axis=0)
    totals = jnp.sum(all_ref[:, 2:] * jnp.exp(all_ref[:, :2] - tops), axis=0)
    factors = jnp.exp(stats_ref[:2] - tops) / totals
    student_factor = jnp.transpose(jnp.broadcast_to(factors[0:1], (rows, rows)))
    teacher_factor = jnp.transpose(jnp.broadcast_to(factors[1:2], (rows, rows)))
    for i in range(student_exp.shape[1] // rows):
        part = slice(i * rows, (i + 1) * rows)
        difference[:, part] = (
            student_exp[:, part] * student_factor - teacher_exp[:, part] * teacher_factor
        ).astype(difference.dtype)

    @pl.loop(0, out.shape[1] // WIDE)
    def _(i):
        part = pl.ds(pl.multiple_of(i * WIDE, WIDE), WIDE)
        out[:, part] = jnp.dot(
            difference[...], head[:, part], preferred_element_type=jnp.float32
        ).astype(out.dtype)


def partial(student_exp, teacher_exp, stats, stats_of, head):
    rows, entries = student_exp.shape
    return pl.pallas_call(
        partial_kernel,
        out_shape=jax.ShapeDtypeStruct((rows, head.shape[1]), jnp.bfloat16),
        in_specs=[IN_VMEM] * 5,
        out_specs=IN_VMEM,
        scratch_shapes=[pltpu.VMEM((rows, entries), jnp.bfloat16)],
        compiler_params=pltpu.CompilerParams(vmem_limit_bytes=12 * MIB),
    )(student_exp, teacher_exp, stats, stats_of, near(head))


def local(student_hidden, teacher_hidden, student_head, teacher_head, row_weight):
    ds, dt = student_hidden.shape[1], teacher_hidden.shape[1]
    mine = jnp.concatenate([student_hidden, teacher_hidden], axis=1)
    far = to_all(mine, FAR, H)
    every = lax.all_to_all(spread(far), NEAR, 0, 0).reshape(Y * Z * 2, ds + dt)
    student_exp, teacher_exp, stats, student_near = logits(every, student_head, teacher_head)
    stats_of = to_all(stats, ALL, Y * Z)
    sums = partial(student_exp, teacher_exp, stats, stats_of, student_near)
    near_sums = lax.all_to_all(sums.reshape(Y * L, H * 2, ds), NEAR, 0, 0)
    far_sums = lax.all_to_all(fold(near_sums), FAR, 0, 0)
    summed = jnp.sum(far_sums.astype(jnp.float32), axis=0)
    return (row_weight[:, None] * summed).astype(jnp.bfloat16)


def solution(mesh):
    split = Mesh(mesh.devices.reshape(-1, Y, H, L), ("grp", "y", "h", "l"))
    rows = P(("grp", *ALL))
    head = P(ALL)
    return jax.shard_map(
        local, mesh=split, in_specs=(rows, rows, head, head, rows), out_specs=rows, check_vma=False
    )
```

time: 169 us -> 153 us (0.905)
  matrix products: 23.6 us -> 0 us
  Pallas kernels: 0 us -> 21.1 us
  waiting for transfers between devices: 17.9 us -> 0 us
  blocking collectives: 113 us -> 129 us
  starting transfers between devices: 8 us -> 0 us
  local copies, waits for them, and re-layouts: 3.02 us -> 0.18 us
    all_to_all x2 -> x3, blocking collectives: 37.6 us -> 67.7 us  [the longest x1 30.2 us: local(): every = lax.all_to_all(spread(far), NEAR, 0, 0).reshape(Y * Z * 2, ds + dt)]
    dot_general x3 -> x0, matrix products: 23.6 us -> none  [the longest x1 9.21 us: local(): lax.dot_general(student_rows, student_head, DIMS, preferred_element_type=...]
    pallas_call x0 -> x4, Pallas kernels: none -> 21.1 us  [the longest x1 16.8 us: logits(): pl.pallas_call(logits_kernel, out_shape=(jax.ShapeDtypeStruct((rows, entr...]
    all_to_all x2 -> x0, waiting for transfers between devices: 17.9 us -> none  [to_all(): lax.all_to_all(jnp.broadcast_to(x[None], (size, *x.shape)), axis, 0, 0)]
    all_to_all x2, blocking collectives: 75.4 us -> 61.5 us  [to_all(): lax.all_to_all(jnp.broadcast_to(x[None], (size, *x.shape)), axis, 0, 0)]
    all_to_all x2 -> x0, starting transfers between devices: 8 us -> none  [to_all(): lax.all_to_all(jnp.broadcast_to(x[None], (size, *x.shape)), axis, 0, 0)]
    broadcast_in_dim x4 -> x2, local copies, waits for them, and re-layouts: 2.62 us -> 0.17 us  [to_all(): jnp.broadcast_to(x[None], (size, *x.shape))]
  transfers between devices with their start and end apart: 2 -> 0, of which waited for: 2 -> 0; matrix products, arithmetic and copies ran while one was open for 5% -> 0% of each run, Pallas kernels for 0% -> 0%
where the time goes in v2:
time: 153 us; the launch traced here: 152 us
  blocking collectives  129 us (84%)
  Pallas kernels  21.1 us (14%)
  other arithmetic  1.61 us (1%)
    all_to_all x2, blocking collectives, to_all(): lax.all_to_all(jnp.broadcast_to(x[None], (size, *x.shape)), axis, 0, 0)  61.5 us
    all_to_all x1, blocking collectives, local(): every = lax.all_to_all(spread(far), NEAR, 0, 0).reshape(Y * Z * 2, ds + dt)  30.2 us
    all_to_all x1, blocking collectives, local(): near_sums = lax.all_to_all(sums.reshape(Y * L, H * 2, ds), NEAR, 0, 0)  19.4 us
    all_to_all x1, blocking collectives, local(): far_sums = lax.all_to_all(fold(near_sums), FAR, 0, 0)  18 us
    pallas_call x1, Pallas kernels, logits(): pl.pallas_call(logits_kernel, out_shape=(jax.ShapeDtypeStruct((rows, entr...  16.8 us
    pallas_call x1, Pallas kernels, partial(): pl.pallas_call(partial_kernel, out_shape=jax.ShapeDtypeStruct((rows, head...  3.89 us

profile of v2, /device:TPU:6, one launch (start us, length us, event | category | flops | bytes accessed | tf_op | source)
XLA Modules:
  0.0 152.2 jit_solution(1069881076235917590)
XLA Ops:
  0.0 0.8 pad_maximum_fusion
  0.8 0.2 broadcast_in_dim.4
  0.9 38.0 %all_to_all.25.far_ref = bf16[8,2,9216]{2,1,0:T(2,128)(2,1)S(1)} all-to-all(bf16[8,2,9216]{2,1,0:T(2,128)(2,1)S(1)} %broadcast_in_dim.4), channel_id=1, replica_groups=mesh['grp'=8,'y'=4,'h'=8,'l'=2] {'h'}, dimensions={0} | all-to-all | bytes 589824 | tf_op jit(solution)/shard_map/all_to_all | solution.py:19
  38.9 0.2 shard_map.55
  39.1 30.2 %all_to_all.26 = bf16[8,16,9216]{2,1,0:T(8,128)(2,1)S(1)} all-to-all(bf16[8,16,9216]{2,1,0:T(8,128)(2,1)S(1)} %shard_map.55), channel_id=1, replica_groups=mesh['grp'=8,'y'=4,'h'=8,'l'=2] {'y','l'}, dimensions={0} | all-to-all | bytes 4718592 | tf_op jit(solution)/shard_map/all_to_all | solution.py:159
  69.4 16.8 %shard_map.56 = (f32[128,1280]{1,0:T(8,128)S(1)}, f32[128,1280]{1,0:T(8,128)S(1)}, f32[4,128]{1,0:T(4,128)S(1)}, bf16[1280,5120]{1,0:T(8,128)(2,1)S(1)}) custom-call(bf16[128,9216]{1,0:T(8,128)(2,1)S(1)} %bitcast.2, bf16[1280,5120]{1,0:T(8,128)(2,1)} %student_far.1, bf16[1280,4096]{1,0:T(8,128)(2,1)} %teacher_far.1), custom_call_target="tpu_custom_call" | custom-call | tf_op jit(solution)/shard_map/pallas_call | solution.py:104
  86.2 23.6 %all_to_all.27.all_ref = f32[64,4,128]{2,1,0:T(4,128)S(1)} all-to-all(f32[64,4,128]{2,1,0:T(4,128)S(1)} %broadcast_in_dim.5), channel_id=1, replica_groups=mesh['grp'=8,'y'=4,'h'=8,'l'=2] {'y','h','l'}, dimensions={0} | all-to-all | bytes 262144 | tf_op jit(solution)/shard_map/all_to_all | solution.py:19
  109.8 3.9 %shard_map.57 = bf16[128,5120]{1,0:T(8,128)(2,1)S(1)} custom-call(f32[128,1280]{1,0:T(8,128)S(1)} %get-tuple-element.9.student_exp, f32[128,1280]{1,0:T(8,128)S(1)} %get-tuple-element.10.teacher_exp, f32[4,128]{1,0:T(4,128)S(1)} %get-tuple-element.11.stats_ref, f32[64,4,128]{2,1,0:T(4,128)S(1)} %all_to_all.27.all_ref, ...), custom_call_target="tpu_custom_call" | custom-call | tf_op jit(solution)/shard_map/pallas_call | solution.py:145
  113.7 0.0 copy-start
  113.7 19.4 %all_to_all.28.sums_ref = bf16[8,16,5120]{2,1,0:T(8,128)(2,1)S(1)} all-to-all(bf16[8,16,5120]{2,1,0:T(8,128)(2,1)S(1)} %bitcast.3), channel_id=1, replica_groups=mesh['grp'=8,'y'=4,'h'=8,'l'=2] {'y','l'}, dimensions={0} | all-to-all | bytes 2621440 | tf_op jit(solution)/shard_map/all_to_all | solution.py:163
  133.1 0.2 shard_map.58
  133.3 18.0 %all_to_all.29 = bf16[8,2,5120]{2,1,0:T(2,128)(2,1)S(1)} all-to-all(bf16[8,2,5120]{2,1,0:T(2,128)(2,1)S(1)} %shard_map.58), channel_id=1, replica_groups=mesh['grp'=8,'y'=4,'h'=8,'l'=2] {'h'}, dimensions={0} | all-to-all | bytes 327680 | tf_op jit(solution)/shard_map/all_to_all | solution.py:164
  151.4 0.1 convert_reduce_fusion
  151.5 0.0 copy-done
  151.5 0.7 multiply_convert_fusion
  (1 shorter events, 0.0 us)
Async XLA Ops:
  113.7 37.8 %copy-start = (f32[2]{0:T(128)S(1)}, f32[2]{0:T(128)}, u32[]{:S(2)}) copy-start(f32[2]{0:T(128)} %param.9) | copy-start | bytes 28

commit v3 on v2

--- a/solution.py
+++ b/solution.py
@@ -10,7 +10,7 @@
 NEAR, FAR, ALL = ("y", "l"), "h", ("y", "h", "l")
 DIMS = (((1,), (1,)), ((), ()))
 MIB = 1 << 20
-WIDE, DEEP = 512, 256
+WIDE, DEEP = 512, 640
 IN_VMEM = pl.BlockSpec(memory_space=pltpu.VMEM)
 IN_HBM = pl.BlockSpec(memory_space=pltpu.HBM)
 
@@ -27,22 +27,22 @@
     return pltpu.with_memory_space_constraint(x, pltpu.VMEM)
 
 
-def spread_kernel(far_ref, out_ref):
+def spread_kernel(far_ref, student_head, teacher_head, out_ref):
     far = far_ref[...].astype(jnp.float32)
     block = jnp.concatenate([far[i] for i in range(far.shape[0])], axis=0).astype(out_ref.dtype)
     for i in range(out_ref.shape[0]):
         out_ref[i] = block
 
 
-def spread(far):
+def spread(far, student_head, teacher_head):
     count, rows, width = far.shape
     return pl.pallas_call(
         spread_kernel,
         out_shape=jax.ShapeDtypeStruct((Y * L, count * rows, width), far.dtype),
-        in_specs=[IN_VMEM],
+        in_specs=[IN_VMEM, IN_HBM, IN_HBM],
         out_specs=IN_VMEM,
         compiler_params=pltpu.CompilerParams(vmem_limit_bytes=8 * MIB),
-    )(far)
+    )(far, far_off(student_head), far_off(teacher_head))
 
 
 def fold_kernel(sums_ref, out_ref):
@@ -62,41 +62,29 @@
     )(sums)
 
 
-def logits_kernel(
-    rows_ref, student_far, teacher_far, student_exp, teacher_exp, stats_ref, student_near, teacher_near, sems
-):
+def logits_kernel(rows_ref, student_ref, teacher_ref, student_exp, teacher_exp, stats_ref, scratch):
     rows = rows_ref.shape[0]
-    pieces = student_far.shape[0] // DEEP
-    heads = ((student_far, student_near, student_exp), (teacher_far, teacher_near, teacher_exp))
-
-    def copy(k, i):
-        part = pl.ds(i * DEEP, DEEP)
-        return pltpu.make_async_copy(heads[k][0].at[part], heads[k][1].at[part], sems.at[k, i])
-
-    for k in range(2):
-        for i in range(pieces):
-            copy(k, i).start()
-    lane = lax.broadcasted_iota(jnp.int32, (rows, rows), 1)
-    stats = jnp.zeros((rows, rows), jnp.float32)
     first = 0
-    for k, (_, head, out) in enumerate(heads):
-        width = head.shape[1]
+    for k, (head, out) in enumerate(((student_ref, student_exp), (teacher_ref, teacher_exp))):
+        entries, width = head.shape
         top = None
-        for i in range(pieces):
-            copy(k, i).wait()
+        for i in range(entries // DEEP):
             part = slice(i * DEEP, (i + 1) * DEEP)
             piece = lax.dot_general(
-                rows_ref[:, first : first + width], head[part, :], DIMS, preferred_element_type=jnp.float32
+                head[part, :], rows_ref[:, first : first + width], DIMS, preferred_element_type=jnp.float32
             )
-            out[:, part] = piece
-            most = jnp.max(piece, axis=1, keepdims=True)
+            scratch[part, :] = piece
+            most = jnp.max(piece, axis=0, keepdims=True)
             top = most if top is None else jnp.maximum(top, most)
-        exp = jnp.exp(out[...] - top)
-        out[...] = exp
-        total = jnp.sum(exp, axis=1, keepdims=True)
-        stats = jnp.where(lane == k, top, jnp.where(lane == 2 + k, total, stats))
+        total = jnp.zeros_like(top)
+        for i in range(entries // rows):
+            part = slice(i * rows, (i + 1) * rows)
+            exp = jnp.exp(scratch[part, :] - top)
+            total += jnp.sum(exp, axis=0, keepdims=True)
+            out[:, part] = jnp.transpose(exp)
+        stats_ref[k : k + 1] = top
+        stats_ref[2 + k : 3 + k] = total
         first += width
-    stats_ref[...] = jnp.transpose(stats)[:4]
 
 
 def logits(every, student_head, teacher_head):
@@ -107,16 +95,12 @@
             jax.ShapeDtypeStruct((rows, entries), jnp.float32),
             jax.ShapeDtypeStruct((rows, entries), jnp.float32),
             jax.ShapeDtypeStruct((4, rows), jnp.float32),
-            pltpu.VMEM(student_head.shape, student_head.dtype),
         ),
-        in_specs=[IN_VMEM, IN_HBM, IN_HBM],
-        out_specs=[IN_VMEM] * 4,
-        scratch_shapes=[
-            pltpu.VMEM(teacher_head.shape, teacher_head.dtype),
-            pltpu.SemaphoreType.DMA((2, entries // DEEP)),
-        ],
-        compiler_params=pltpu.CompilerParams(vmem_limit_bytes=24 * MIB),
-    )(every, far_off(student_head), far_off(teacher_head))
+        in_specs=[IN_VMEM] * 3,
+        out_specs=[IN_VMEM] * 3,
+        scratch_shapes=[pltpu.VMEM((entries, rows), jnp.float32)],
+        compiler_params=pltpu.CompilerParams(vmem_limit_bytes=12 * MIB),
+    )(every, near(student_head), near(teacher_head))
 
 
 def partial_kernel(student_exp, teacher_exp, stats_ref, all_ref, head, out, difference):
@@ -156,10 +140,10 @@
     ds, dt = student_hidden.shape[1], teacher_hidden.shape[1]
     mine = jnp.concatenate([student_hidden, teacher_hidden], axis=1)
     far = to_all(mine, FAR, H)
-    every = lax.all_to_all(spread(far), NEAR, 0, 0).reshape(Y * Z * 2, ds + dt)
-    student_exp, teacher_exp, stats, student_near = logits(every, student_head, teacher_head)
+    every = lax.all_to_all(spread(far, student_head, teacher_head), NEAR, 0, 0).reshape(Y * Z * 2, ds + dt)
+    student_exp, teacher_exp, stats = logits(every, student_head, teacher_head)
     stats_of = to_all(stats, ALL, Y * Z)
-    sums = partial(student_exp, teacher_exp, stats, stats_of, student_near)
+    sums = partial(student_exp, teacher_exp, stats, stats_of, student_head)
     near_sums = lax.all_to_all(sums.reshape(Y * L, H * 2, ds), NEAR, 0, 0)
     far_sums = lax.all_to_all(fold(near_sums), FAR, 0, 0)
     summed = jnp.sum(far_sums.astype(jnp.float32), axis=0)

time: 153 us -> 143 us (0.935)
  Pallas kernels: 21.1 us -> 10.9 us
    pallas_call x1, Pallas kernels: 16.8 us -> 6.58 us  [logits(): pl.pallas_call(logits_kernel, out_shape=(jax.ShapeDtypeStruct((rows, entr...]
where the time goes in v3:
time: 143 us
  blocking collectives  130 us (91%)
  Pallas kernels  10.9 us (8%)
  other arithmetic  1.61 us (1%)
    all_to_all x2, blocking collectives, to_all(): lax.all_to_all(jnp.broadcast_to(x[None], (size, *x.shape)), axis, 0, 0)  61.8 us
    all_to_all x1, blocking collectives, local(): lax.all_to_all(spread(far, student_head, teacher_head), NEAR, 0, 0)  30.5 us
    all_to_all x1, blocking collectives, local(): near_sums = lax.all_to_all(sums.reshape(Y * L, H * 2, ds), NEAR, 0, 0)  19.4 us
    all_to_all x1, blocking collectives, local(): far_sums = lax.all_to_all(fold(near_sums), FAR, 0, 0)  18 us
    pallas_call x1, Pallas kernels, logits(): pl.pallas_call(logits_kernel, out_shape=(jax.ShapeDtypeStruct((rows, entr...  6.58 us
    pallas_call x1, Pallas kernels, partial(): pl.pallas_call(partial_kernel, out_shape=jax.ShapeDtypeStruct((rows, head...  3.89 us

profile of v3, /device:TPU:6, one launch (start us, length us, event | category | flops | bytes accessed | tf_op | source)
XLA Modules:
  0.0 142.5 jit_solution(3105415061520722508)
XLA Ops:
  0.0 0.8 pad_maximum_fusion
  0.8 0.2 broadcast_in_dim.4
  0.9 0.0 slice-start
  1.0 38.2 %all_to_all.25.far_ref = bf16[8,2,9216]{2,1,0:T(2,128)(2,1)S(1)} all-to-all(bf16[8,2,9216]{2,1,0:T(2,128)(2,1)S(1)} %broadcast_in_dim.4), channel_id=1, replica_groups=mesh['grp'=8,'y'=4,'h'=8,'l'=2] {'h'}, dimensions={0} | all-to-all | bytes 589824 | tf_op jit(solution)/shard_map/all_to_all | solution.py:19
  39.2 0.0 slice-start.1
  39.2 0.0 slice-start.2
  39.2 0.0 slice-start.3
  39.2 0.0 copy-start
  39.2 0.2 shard_map.55
  39.4 30.5 %all_to_all.26 = bf16[8,16,9216]{2,1,0:T(8,128)(2,1)S(1)} all-to-all(bf16[8,16,9216]{2,1,0:T(8,128)(2,1)S(1)} %shard_map.55), channel_id=1, replica_groups=mesh['grp'=8,'y'=4,'h'=8,'l'=2] {'y','l'}, dimensions={0} | all-to-all | bytes 4718592 | tf_op jit(solution)/shard_map/all_to_all | solution.py:143
  69.9 0.0 slice-done
  69.9 0.0 slice-done.1
  69.9 0.0 slice-done.2
  69.9 0.0 slice-done.3
  69.9 0.0 copy-done
  70.0 6.6 %shard_map.56 = (f32[128,1280]{1,0:T(8,128)S(1)}, f32[128,1280]{1,0:T(8,128)S(1)}, f32[4,128]{1,0:T(4,128)S(1)}) custom-call(bf16[128,9216]{1,0:T(8,128)(2,1)S(1)} %bitcast.4, bf16[1280,5120]{1,0:T(8,128)(2,1)S(1)} %bitcast.3, bf16[1280,4096]{1,0:T(8,128)(2,1)S(1)} %copy-done), custom_call_target="tpu_custom_call" | custom-call | tf_op jit(solution)/shard_map/pallas_call | solution.py:92
  76.6 23.6 %all_to_all.27.all_ref = f32[64,4,128]{2,1,0:T(4,128)S(1)} all-to-all(f32[64,4,128]{2,1,0:T(4,128)S(1)} %broadcast_in_dim.5), channel_id=1, replica_groups=mesh['grp'=8,'y'=4,'h'=8,'l'=2] {'y','h','l'}, dimensions={0} | all-to-all | bytes 262144 | tf_op jit(solution)/shard_map/all_to_all | solution.py:19
  100.1 3.9 %shard_map.57 = bf16[128,5120]{1,0:T(8,128)(2,1)S(1)} custom-call(f32[128,1280]{1,0:T(8,128)S(1)} %get-tuple-element.8.student_exp, f32[128,1280]{1,0:T(8,128)S(1)} %get-tuple-element.9.teacher_exp, f32[4,128]{1,0:T(4,128)S(1)} %get-tuple-element.10.stats_ref, f32[64,4,128]{2,1,0:T(4,128)S(1)} %all_to_all.27.all_ref, bf16[1280,5120]{1,0:T(8,128)(2,1)S(1)} %bitcast.3), custom_call_target="tpu_custom_call" | custom-call | tf_op jit(solution)/shard_map/pallas_call | solution.py:129
  104.0 0.0 copy-start.1
  104.1 19.4 %all_to_all.28.sums_ref = bf16[8,16,5120]{2,1,0:T(8,128)(2,1)S(1)} all-to-all(bf16[8,16,5120]{2,1,0:T(8,128)(2,1)S(1)} %bitcast.5), channel_id=1, replica_groups=mesh['grp'=8,'y'=4,'h'=8,'l'=2] {'y','l'}, dimensions={0} | all-to-all | bytes 2621440 | tf_op jit(solution)/shard_map/all_to_all | solution.py:147
  123.5 0.2 shard_map.58
  123.7 18.0 %all_to_all.29 = bf16[8,2,5120]{2,1,0:T(2,128)(2,1)S(1)} all-to-all(bf16[8,2,5120]{2,1,0:T(2,128)(2,1)S(1)} %shard_map.58), channel_id=1, replica_groups=mesh['grp'=8,'y'=4,'h'=8,'l'=2] {'h'}, dimensions={0} | all-to-all | bytes 327680 | tf_op jit(solution)/shard_map/all_to_all | solution.py:148
  141.7 0.1 convert_reduce_fusion
  141.8 0.0 copy-done.1
  141.8 0.7 multiply_convert_fusion
  (2 shorter events, 0.0 us)
Async XLA Ops:
  0.9 69.0 %slice-start = ((s8[13107200]{0:T(1024)(128)(4,1)}), s8[4194304]{0:T(1024)(128)(4,1)S(1)}, s32[]{:S(2)}) async-start(s8[13107200]{0:T(1024)(128)(4,1)} %bitcast.2), calls=%async_computation.5 | async-start | bytes 8388608
  39.2 30.7 %slice-start.1 = ((s8[13107200]{0:T(1024)(128)(4,1)}), s8[4194304]{0:T(1024)(128)(4,1)S(1)}, s32[]{:S(2)}) async-start(s8[13107200]{0:T(1024)(128)(4,1)} %bitcast.2), calls=%async_computation.6 | async-start | bytes 8388608
  39.2 30.7 %slice-start.2 = ((s8[13107200]{0:T(1024)(128)(4,1)}), s8[4194304]{0:T(1024)(128)(4,1)S(1)}, s32[]{:S(2)}) async-start(s8[13107200]{0:T(1024)(128)(4,1)} %bitcast.2), calls=%async_computation.7 | async-start | bytes 8388608
  39.2 30.7 %slice-start.3 = ((s8[13107200]{0:T(1024)(128)(4,1)}), s8[524288]{0:T(1024)(128)(4,1)S(1)}, s32[]{:S(2)}) async-start(s8[13107200]{0:T(1024)(128)(4,1)} %bitcast.2), calls=%async_computation.8 | async-start | bytes 1048576
  39.2 30.7 %copy-start = (bf16[1280,4096]{1,0:T(8,128)(2,1)S(1)}, bf16[1280,4096]{1,0:T(8,128)(2,1)}, u32[]{:S(2)}) copy-start(bf16[1280,4096]{1,0:T(8,128)(2,1)} %teacher_ref.1) | copy-start | bytes 31457284
  104.0 37.8 %copy-start.1 = (f32[2]{0:T(128)S(1)}, f32[2]{0:T(128)}, u32[]{:S(2)}) copy-start(f32[2]{0:T(128)} %param.9) | copy-start | bytes 28

commit v4 on v3

--- a/solution.py
+++ b/solution.py
@@ -10,7 +10,7 @@
 NEAR, FAR, ALL = ("y", "l"), "h", ("y", "h", "l")
 DIMS = (((1,), (1,)), ((), ()))
 MIB = 1 << 20
-WIDE, DEEP = 512, 640
+WIDE, DEEP = 2560, 256
 IN_VMEM = pl.BlockSpec(memory_space=pltpu.VMEM)
 IN_HBM = pl.BlockSpec(memory_space=pltpu.HBM)
 
@@ -62,7 +62,23 @@
     )(sums)
 
 
-def logits_kernel(rows_ref, student_ref, teacher_ref, student_exp, teacher_exp, stats_ref, scratch):
+def finish_kernel(sums_ref, weight_ref, out_ref):
+    summed = jnp.sum(sums_ref[...].astype(jnp.float32), axis=0)
+    row = lax.broadcasted_iota(jnp.int32, summed.shape, 0)
+    out_ref[...] = (jnp.where(row == 0, weight_ref[0], weight_ref[1]) * summed).astype(out_ref.dtype)
+
+
+def finish(sums, row_weight):
+    return pl.pallas_call(
+        finish_kernel,
+        out_shape=jax.ShapeDtypeStruct(sums.shape[1:], sums.dtype),
+        in_specs=[IN_VMEM, pl.BlockSpec(memory_space=pltpu.SMEM)],
+        out_specs=IN_VMEM,
+        compiler_params=pltpu.CompilerParams(vmem_limit_bytes=4 * MIB),
+    )(sums, row_weight)
+
+
+def logits_kernel(rows_ref, student_ref, teacher_ref, student_exp, teacher_exp, tops_ref, sums_ref, scratch):
     rows = rows_ref.shape[0]
     first = 0
     for k, (head, out) in enumerate(((student_ref, student_exp), (teacher_ref, teacher_exp))):
@@ -82,8 +98,8 @@
             exp = jnp.exp(scratch[part, :] - top)
             total += jnp.sum(exp, axis=0, keepdims=True)
             out[:, part] = jnp.transpose(exp)
-        stats_ref[k : k + 1] = top
-        stats_ref[2 + k : 3 + k] = total
+        tops_ref[k : k + 1] = top
+        sums_ref[k : k + 1] = top + jnp.log(total)
         first += width
 
 
@@ -94,20 +110,21 @@
         out_shape=(
             jax.ShapeDtypeStruct((rows, entries), jnp.float32),
             jax.ShapeDtypeStruct((rows, entries), jnp.float32),
-            jax.ShapeDtypeStruct((4, rows), jnp.float32),
+            jax.ShapeDtypeStruct((2, rows), jnp.float32),
+            jax.ShapeDtypeStruct((2, rows), jnp.float32),
         ),
         in_specs=[IN_VMEM] * 3,
-        out_specs=[IN_VMEM] * 3,
+        out_specs=[IN_VMEM] * 4,
         scratch_shapes=[pltpu.VMEM((entries, rows), jnp.float32)],
         compiler_params=pltpu.CompilerParams(vmem_limit_bytes=12 * MIB),
     )(every, near(student_head), near(teacher_head))
 
 
-def partial_kernel(student_exp, teacher_exp, stats_ref, all_ref, head, out, difference):
+def partial_kernel(student_exp, teacher_exp, tops_ref, all_ref, head, out, difference):
     rows = student_exp.shape[0]
-    tops = jnp.max(all_ref[:, :2], axis=0)
-    totals = jnp.sum(all_ref[:, 2:] * jnp.exp(all_ref[:, :2] - tops), axis=0)
-    factors = jnp.exp(stats_ref[:2] - tops) / totals
+    most = jnp.max(all_ref[...], axis=0)
+    total = jnp.sum(jnp.exp(all_ref[...] - most), axis=0)
+    factors = jnp.exp(tops_ref[...] - most) / total
     student_factor = jnp.transpose(jnp.broadcast_to(factors[0:1], (rows, rows)))
     teacher_factor = jnp.transpose(jnp.broadcast_to(factors[1:2], (rows, rows)))
     for i in range(student_exp.shape[1] // rows):
@@ -116,15 +133,14 @@
             student_exp[:, part] * student_factor - teacher_exp[:, part] * teacher_factor
         ).astype(difference.dtype)
 
-    @pl.loop(0, out.shape[1] // WIDE)
-    def _(i):
-        part = pl.ds(pl.multiple_of(i * WIDE, WIDE), WIDE)
+    for i in range(out.shape[1] // WIDE):
+        part = slice(i * WIDE, (i + 1) * WIDE)
         out[:, part] = jnp.dot(
             difference[...], head[:, part], preferred_element_type=jnp.float32
         ).astype(out.dtype)
 
 
-def partial(student_exp, teacher_exp, stats, stats_of, head):
+def partial(student_exp, teacher_exp, tops, sums_of, head):
     rows, entries = student_exp.shape
     return pl.pallas_call(
         partial_kernel,
@@ -133,7 +149,7 @@
         out_specs=IN_VMEM,
         scratch_shapes=[pltpu.VMEM((rows, entries), jnp.bfloat16)],
         compiler_params=pltpu.CompilerParams(vmem_limit_bytes=12 * MIB),
-    )(student_exp, teacher_exp, stats, stats_of, near(head))
+    )(student_exp, teacher_exp, tops, sums_of, near(head))
 
 
 def local(student_hidden, teacher_hidden, student_head, teacher_head, row_weight):
@@ -141,13 +157,12 @@
     mine = jnp.concatenate([student_hidden, teacher_hidden], axis=1)
     far = to_all(mine, FAR, H)
     every = lax.all_to_all(spread(far, student_head, teacher_head), NEAR, 0, 0).reshape(Y * Z * 2, ds + dt)
-    student_exp, teacher_exp, stats = logits(every, student_head, teacher_head)
-    stats_of = to_all(stats, ALL, Y * Z)
-    sums = partial(student_exp, teacher_exp, stats, stats_of, student_head)
-    near_sums = lax.all_to_all(sums.reshape(Y * L, H * 2, ds), NEAR, 0, 0)
+    student_exp, teacher_exp, tops, log_sums = logits(every, student_head, teacher_head)
+    log_sums_of = to_all(log_sums, ALL, Y * Z)
+    parts = partial(student_exp, teacher_exp, tops, log_sums_of, student_head)
+    near_sums = lax.all_to_all(parts.reshape(Y * L, H * 2, ds), NEAR, 0, 0)
     far_sums = lax.all_to_all(fold(near_sums), FAR, 0, 0)
-    summed = jnp.sum(far_sums.astype(jnp.float32), axis=0)
-    return (row_weight[:, None] * summed).astype(jnp.bfloat16)
+    return finish(far_sums, row_weight)
 
 
 def solution(mesh):

time: 143 us -> 141 us (0.986)
    pallas_call x1, Pallas kernels: 3.89 us -> 2.21 us  [partial(): pl.pallas_call(partial_kernel, out_shape=jax.ShapeDtypeStruct((rows, head...]
where the time goes in v4:
time: 141 us; the launch traced here: 140 us
  blocking collectives  129 us (91%)
  Pallas kernels  10.5 us (7%)
    all_to_all x2, blocking collectives, to_all(): lax.all_to_all(jnp.broadcast_to(x[None], (size, *x.shape)), axis, 0, 0)  61.4 us
    all_to_all x1, blocking collectives, local(): lax.all_to_all(spread(far, student_head, teacher_head), NEAR, 0, 0)  30.5 us
    all_to_all x1, blocking collectives, local(): near_sums = lax.all_to_all(parts.reshape(Y * L, H * 2, ds), NEAR, 0, 0)  18.7 us
    all_to_all x1, blocking collectives, local(): far_sums = lax.all_to_all(fold(near_sums), FAR, 0, 0)  18 us
    pallas_call x1, Pallas kernels, logits(): pl.pallas_call(logits_kernel, out_shape=(jax.ShapeDtypeStruct((rows, entr...  6.59 us

profile of v4, /device:TPU:6, one launch (start us, length us, event | category | flops | bytes accessed | tf_op | source)
XLA Modules:
  0.0 140.1 jit_solution(15578620949973274957)
XLA Ops:
  0.0 0.8 pad_maximum_fusion
  0.8 0.2 broadcast_in_dim.4
  0.9 0.0 slice-start
  1.0 38.2 %all_to_all.25.far_ref = bf16[8,2,9216]{2,1,0:T(2,128)(2,1)S(1)} all-to-all(bf16[8,2,9216]{2,1,0:T(2,128)(2,1)S(1)} %broadcast_in_dim.4), channel_id=1, replica_groups=mesh['grp'=8,'y'=4,'h'=8,'l'=2] {'h'}, dimensions={0} | all-to-all | bytes 589824 | tf_op jit(solution)/shard_map/all_to_all | solution.py:19
  39.2 0.0 slice-start.1
  39.2 0.0 slice-start.2
  39.2 0.0 slice-start.3
  39.2 0.0 copy-start
  39.2 0.2 shard_map.55
  39.4 30.5 %all_to_all.26 = bf16[8,16,9216]{2,1,0:T(8,128)(2,1)S(1)} all-to-all(bf16[8,16,9216]{2,1,0:T(8,128)(2,1)S(1)} %shard_map.55), channel_id=1, replica_groups=mesh['grp'=8,'y'=4,'h'=8,'l'=2] {'y','l'}, dimensions={0} | all-to-all | bytes 4718592 | tf_op jit(solution)/shard_map/all_to_all | solution.py:159
  69.9 0.0 slice-done
  69.9 0.0 slice-done.1
  69.9 0.0 slice-done.2
  69.9 0.0 slice-done.3
  69.9 0.0 copy-done
  70.0 6.6 %shard_map.56 = (f32[128,1280]{1,0:T(8,128)S(1)}, f32[128,1280]{1,0:T(8,128)S(1)}, f32[2,128]{1,0:T(2,128)S(1)}, f32[2,128]{1,0:T(2,128)S(1)}) custom-call(bf16[128,9216]{1,0:T(8,128)(2,1)S(1)} %bitcast.4, bf16[1280,5120]{1,0:T(8,128)(2,1)S(1)} %bitcast.3, bf16[1280,4096]{1,0:T(8,128)(2,1)S(1)} %copy-done), custom_call_target="tpu_custom_call" | custom-call | tf_op jit(solution)/shard_map/pallas_call | solution.py:108
  76.6 23.1 %all_to_all.27.all_ref = f32[64,2,128]{2,1,0:T(2,128)S(1)} all-to-all(f32[64,2,128]{2,1,0:T(2,128)S(1)} %broadcast_in_dim.5), channel_id=1, replica_groups=mesh['grp'=8,'y'=4,'h'=8,'l'=2] {'y','h','l'}, dimensions={0} | all-to-all | bytes 131072 | tf_op jit(solution)/shard_map/all_to_all | solution.py:19
  99.7 2.2 %shard_map.57 = bf16[128,5120]{1,0:T(8,128)(2,1)S(1)} custom-call(f32[128,1280]{1,0:T(8,128)S(1)} %get-tuple-element.9.student_exp, f32[128,1280]{1,0:T(8,128)S(1)} %get-tuple-element.10.teacher_exp, f32[2,128]{1,0:T(2,128)S(1)} %get-tuple-element.11.tops_ref, f32[64,2,128]{2,1,0:T(2,128)S(1)} %all_to_all.27.all_ref, bf16[1280,5120]{1,0:T(8,128)(2,1)S(1)} %bitcast.3), custom_call_target="tpu_custom_call" | custom-call | tf_op jit(solution)/shard_map/pallas_call | solution.py:145
  101.9 0.0 copy-start.1
  101.9 18.7 %all_to_all.28.sums_ref = bf16[8,16,5120]{2,1,0:T(8,128)(2,1)S(1)} all-to-all(bf16[8,16,5120]{2,1,0:T(8,128)(2,1)S(1)} %bitcast.5), channel_id=1, replica_groups=mesh['grp'=8,'y'=4,'h'=8,'l'=2] {'y','l'}, dimensions={0} | all-to-all | bytes 2621440 | tf_op jit(solution)/shard_map/all_to_all | solution.py:163
  120.6 0.2 shard_map.58
  120.8 18.0 %all_to_all.29.sums_ref = bf16[8,2,5120]{2,1,0:T(2,128)(2,1)S(1)} all-to-all(bf16[8,2,5120]{2,1,0:T(2,128)(2,1)S(1)} %shard_map.58), channel_id=1, replica_groups=mesh['grp'=8,'y'=4,'h'=8,'l'=2] {'h'}, dimensions={0} | all-to-all | bytes 327680 | tf_op jit(solution)/shard_map/all_to_all | solution.py:164
  138.8 0.0 copy-done.1
  138.8 1.3 shard_map.59
  (2 shorter events, 0.0 us)
Async XLA Ops:
  0.9 69.0 %slice-start = ((s8[13107200]{0:T(1024)(128)(4,1)}), s8[4194304]{0:T(1024)(128)(4,1)S(1)}, s32[]{:S(2)}) async-start(s8[13107200]{0:T(1024)(128)(4,1)} %bitcast.2), calls=%async_computation.5 | async-start | bytes 8388608
  39.2 30.7 %slice-start.1 = ((s8[13107200]{0:T(1024)(128)(4,1)}), s8[4194304]{0:T(1024)(128)(4,1)S(1)}, s32[]{:S(2)}) async-start(s8[13107200]{0:T(1024)(128)(4,1)} %bitcast.2), calls=%async_computation.6 | async-start | bytes 8388608
  39.2 30.7 %slice-start.2 = ((s8[13107200]{0:T(1024)(128)(4,1)}), s8[4194304]{0:T(1024)(128)(4,1)S(1)}, s32[]{:S(2)}) async-start(s8[13107200]{0:T(1024)(128)(4,1)} %bitcast.2), calls=%async_computation.7 | async-start | bytes 8388608
  39.2 30.7 %slice-start.3 = ((s8[13107200]{0:T(1024)(128)(4,1)}), s8[524288]{0:T(1024)(128)(4,1)S(1)}, s32[]{:S(2)}) async-start(s8[13107200]{0:T(1024)(128)(4,1)} %bitcast.2), calls=%async_computation.8 | async-start | bytes 1048576
  39.2 30.7 %copy-start = (bf16[1280,4096]{1,0:T(8,128)(2,1)S(1)}, bf16[1280,4096]{1,0:T(8,128)(2,1)}, u32[]{:S(2)}) copy-start(bf16[1280,4096]{1,0:T(8,128)(2,1)} %teacher_ref.1) | copy-start | bytes 31457284
  101.9 36.9 %copy-start.1 = (f32[2]{0:T(128)S(1)}, f32[2]{0:T(128)}, u32[]{:S(2)}) copy-start(f32[2]{0:T(128)} %weight_ref.1) | copy-start | bytes 28

commit v5 on v4

--- a/solution.py
+++ b/solution.py
@@ -60,22 +60,6 @@
         out_specs=IN_VMEM,
         compiler_params=pltpu.CompilerParams(vmem_limit_bytes=8 * MIB),
     )(sums)
-
-
-def finish_kernel(sums_ref, weight_ref, out_ref):
-    summed = jnp.sum(sums_ref[...].astype(jnp.float32), axis=0)
-    row = lax.broadcasted_iota(jnp.int32, summed.shape, 0)
-    out_ref[...] = (jnp.where(row == 0, weight_ref[0], weight_ref[1]) * summed).astype(out_ref.dtype)
-
-
-def finish(sums, row_weight):
-    return pl.pallas_call(
-        finish_kernel,
-        out_shape=jax.ShapeDtypeStruct(sums.shape[1:], sums.dtype),
-        in_specs=[IN_VMEM, pl.BlockSpec(memory_space=pltpu.SMEM)],
-        out_specs=IN_VMEM,
-        compiler_params=pltpu.CompilerParams(vmem_limit_bytes=4 * MIB),
-    )(sums, row_weight)
 
 
 def logits_kernel(rows_ref, student_ref, teacher_ref, student_exp, teacher_exp, tops_ref, sums_ref, scratch):
@@ -155,14 +139,15 @@
 def local(student_hidden, teacher_hidden, student_head, teacher_head, row_weight):
     ds, dt = student_hidden.shape[1], teacher_hidden.shape[1]
     mine = jnp.concatenate([student_hidden, teacher_hidden], axis=1)
-    far = to_all(mine, FAR, H)
+    far = lax.all_gather(mine, FAR)
     every = lax.all_to_all(spread(far, student_head, teacher_head), NEAR, 0, 0).reshape(Y * Z * 2, ds + dt)
     student_exp, teacher_exp, tops, log_sums = logits(every, student_head, teacher_head)
     log_sums_of = to_all(log_sums, ALL, Y * Z)
     parts = partial(student_exp, teacher_exp, tops, log_sums_of, student_head)
     near_sums = lax.all_to_all(parts.reshape(Y * L, H * 2, ds), NEAR, 0, 0)
     far_sums = lax.all_to_all(fold(near_sums), FAR, 0, 0)
-    return finish(far_sums, row_weight)
+    summed = jnp.sum(far_sums.astype(jnp.float32), axis=0)
+    return (row_weight[:, None] * summed).astype(jnp.bfloat16)
 
 
 def solution(mesh):

time: 141 us -> 136 us (0.965)
  blocking collectives: 129 us -> 125 us
    all_to_all x2 -> x1, blocking collectives: 61.4 us -> 23.6 us  [to_all(): lax.all_to_all(jnp.broadcast_to(x[None], (size, *x.shape)), axis, 0, 0)]
    all_gather x0 -> x1, blocking collectives: none -> 36 us  [local(): far = lax.all_gather(mine, FAR)]
    all_to_all x1, blocking collectives: 30.5 us -> 28.7 us  [local(): lax.all_to_all(spread(far, student_head, teacher_head), NEAR, 0, 0)]
where the time goes in v5:
time: 136 us
  blocking collectives  125 us (92%)
  Pallas kernels  9.2 us (7%)
  other arithmetic  1.61 us (1%)
    all_gather x1, blocking collectives, local(): far = lax.all_gather(mine, FAR)  36 us
    all_to_all x1, blocking collectives, local(): lax.all_to_all(spread(far, student_head, teacher_head), NEAR, 0, 0)  28.7 us
    all_to_all x1, blocking collectives, to_all(): lax.all_to_all(jnp.broadcast_to(x[None], (size, *x.shape)), axis, 0, 0)  23.6 us
    all_to_all x1, blocking collectives, local(): near_sums = lax.all_to_all(parts.reshape(Y * L, H * 2, ds), NEAR, 0, 0)  19.2 us
    all_to_all x1, blocking collectives, local(): far_sums = lax.all_to_all(fold(near_sums), FAR, 0, 0)  17.6 us
    pallas_call x1, Pallas kernels, logits(): pl.pallas_call(logits_kernel, out_shape=(jax.ShapeDtypeStruct((rows, entr...  6.6 us

profile of v5, /device:TPU:6, one launch (start us, length us, event | category | flops | bytes accessed | tf_op | source)
XLA Modules:
  0.0 136.0 jit_solution(6491151980446719522)
XLA Ops:
  0.0 0.8 maximum_bitcast_fusion
  0.8 0.0 slice-start
  0.8 36.0 %all-gather.1.far_ref = bf16[8,2,9216]{2,1,0:T(2,128)(2,1)S(1)} all-gather(bf16[1,2,9216]{2,1,0:T(2,128)(2,1)S(1)} %maximum_bitcast_fusion), channel_id=2, replica_groups=mesh['grp'=8,'y'=4,'h'=8,'l'=2] {'h'}, dimensions={0}, use_global_device_ids=true | all-gather | bytes 331776 | tf_op jit(solution)/shard_map/all_gather | solution.py:142
  36.8 0.0 slice-start.1
  36.8 0.0 slice-start.2
  36.8 0.0 slice-start.3
  36.8 0.0 copy-start
  36.8 0.2 shard_map.55
  37.0 28.7 %all_to_all.20 = bf16[8,16,9216]{2,1,0:T(8,128)(2,1)S(1)} all-to-all(bf16[8,16,9216]{2,1,0:T(8,128)(2,1)S(1)} %shard_map.55), channel_id=1, replica_groups=mesh['grp'=8,'y'=4,'h'=8,'l'=2] {'y','l'}, dimensions={0} | all-to-all | bytes 4718592 | tf_op jit(solution)/shard_map/all_to_all | solution.py:143
  65.8 0.0 slice-done
  65.8 0.0 slice-done.1
  65.8 0.0 slice-done.2
  65.8 0.0 slice-done.3
  65.8 0.0 copy-done
  65.8 6.6 %shard_map.56 = (f32[128,1280]{1,0:T(8,128)S(1)}, f32[128,1280]{1,0:T(8,128)S(1)}, f32[2,128]{1,0:T(2,128)S(1)}, f32[2,128]{1,0:T(2,128)S(1)}) custom-call(bf16[128,9216]{1,0:T(8,128)(2,1)S(1)} %bitcast.6, bf16[1280,5120]{1,0:T(8,128)(2,1)S(1)} %bitcast.5, bf16[1280,4096]{1,0:T(8,128)(2,1)S(1)} %copy-done), custom_call_target="tpu_custom_call" | custom-call | tf_op jit(solution)/shard_map/pallas_call | solution.py:92
  72.4 23.6 %all_to_all.21.all_ref = f32[64,2,128]{2,1,0:T(2,128)S(1)} all-to-all(f32[64,2,128]{2,1,0:T(2,128)S(1)} %broadcast_in_dim.2), channel_id=1, replica_groups=mesh['grp'=8,'y'=4,'h'=8,'l'=2] {'y','h','l'}, dimensions={0} | all-to-all | bytes 131072 | tf_op jit(solution)/shard_map/all_to_all | solution.py:19
  96.0 2.2 %shard_map.57 = bf16[128,5120]{1,0:T(8,128)(2,1)S(1)} custom-call(f32[128,1280]{1,0:T(8,128)S(1)} %get-tuple-element.9.student_exp, f32[128,1280]{1,0:T(8,128)S(1)} %get-tuple-element.10.teacher_exp, f32[2,128]{1,0:T(2,128)S(1)} %get-tuple-element.11.tops_ref, f32[64,2,128]{2,1,0:T(2,128)S(1)} %all_to_all.21.all_ref, bf16[1280,5120]{1,0:T(8,128)(2,1)S(1)} %bitcast.5), custom_call_target="tpu_custom_call" | custom-call | tf_op jit(solution)/shard_map/pallas_call | solution.py:129
  98.2 0.0 copy-start.1
  98.2 19.2 %all_to_all.22.sums_ref = bf16[8,16,5120]{2,1,0:T(8,128)(2,1)S(1)} all-to-all(bf16[8,16,5120]{2,1,0:T(8,128)(2,1)S(1)} %bitcast.7), channel_id=1, replica_groups=mesh['grp'=8,'y'=4,'h'=8,'l'=2] {'y','l'}, dimensions={0} | all-to-all | bytes 2621440 | tf_op jit(solution)/shard_map/all_to_all | solution.py:147
  117.4 0.2 shard_map.58
  117.6 17.6 %all_to_all.23 = bf16[8,2,5120]{2,1,0:T(2,128)(2,1)S(1)} all-to-all(bf16[8,2,5120]{2,1,0:T(2,128)(2,1)S(1)} %shard_map.58), channel_id=1, replica_groups=mesh['grp'=8,'y'=4,'h'=8,'l'=2] {'h'}, dimensions={0} | all-to-all | bytes 327680 | tf_op jit(solution)/shard_map/all_to_all | solution.py:148
  135.2 0.1 convert_reduce_fusion
  135.3 0.0 copy-done.1
  135.3 0.7 multiply_convert_fusion
  (2 shorter events, 0.0 us)
Async XLA Ops:
  0.8 65.0 %slice-start = ((s8[13107200]{0:T(1024)(128)(4,1)}), s8[4194304]{0:T(1024)(128)(4,1)S(1)}, s32[]{:S(2)}) async-start(s8[13107200]{0:T(1024)(128)(4,1)} %bitcast.4), calls=%async_computation.4 | async-start | bytes 8388608
  36.8 29.0 %slice-start.1 = ((s8[13107200]{0:T(1024)(128)(4,1)}), s8[4194304]{0:T(1024)(128)(4,1)S(1)}, s32[]{:S(2)}) async-start(s8[13107200]{0:T(1024)(128)(4,1)} %bitcast.4), calls=%async_computation.5 | async-start | bytes 8388608
  36.8 29.0 %slice-start.2 = ((s8[13107200]{0:T(1024)(128)(4,1)}), s8[4194304]{0:T(1024)(128)(4,1)S(1)}, s32[]{:S(2)}) async-start(s8[13107200]{0:T(1024)(128)(4,1)} %bitcast.4), calls=%async_computation.6 | async-start | bytes 8388608
  36.8 29.0 %slice-start.3 = ((s8[13107200]{0:T(1024)(128)(4,1)}), s8[524288]{0:T(1024)(128)(4,1)S(1)}, s32[]{:S(2)}) async-start(s8[13107200]{0:T(1024)(128)(4,1)} %bitcast.4), calls=%async_computation.7 | async-start | bytes 1048576
  36.8 29.0 %copy-start = (bf16[1280,4096]{1,0:T(8,128)(2,1)S(1)}, bf16[1280,4096]{1,0:T(8,128)(2,1)}, u32[]{:S(2)}) copy-start(bf16[1280,4096]{1,0:T(8,128)(2,1)} %teacher_ref.1) | copy-start | bytes 31457284
  98.2 37.1 %copy-start.1 = (f32[2]{0:T(128)S(1)}, f32[2]{0:T(128)}, u32[]{:S(2)}) copy-start(f32[2]{0:T(128)} %param.9) | copy-start | bytes 28

commit v6 on v5

--- a/solution.py
+++ b/solution.py
@@ -7,7 +7,7 @@
 
 Y, Z, L = 4, 16, 2
 H = Z // L
-NEAR, FAR, ALL = ("y", "l"), "h", ("y", "h", "l")
+NEAR, FAR, ALL = ("y", "l"), ("b", "a"), ("y", "a", "b", "l")
 DIMS = (((1,), (1,)), ((), ()))
 MIB = 1 << 20
 WIDE, DEEP = 2560, 256
@@ -139,7 +139,7 @@
 def local(student_hidden, teacher_hidden, student_head, teacher_head, row_weight):
     ds, dt = student_hidden.shape[1], teacher_hidden.shape[1]
     mine = jnp.concatenate([student_hidden, teacher_hidden], axis=1)
-    far = lax.all_gather(mine, FAR)
+    far = lax.all_gather(lax.all_gather(mine, "a"), "b").reshape(H, 2, ds + dt)
     every = lax.all_to_all(spread(far, student_head, teacher_head), NEAR, 0, 0).reshape(Y * Z * 2, ds + dt)
     student_exp, teacher_exp, tops, log_sums = logits(every, student_head, teacher_head)
     log_sums_of = to_all(log_sums, ALL, Y * Z)
@@ -151,7 +151,7 @@
 
 
 def solution(mesh):
-    split = Mesh(mesh.devices.reshape(-1, Y, H, L), ("grp", "y", "h", "l"))
+    split = Mesh(mesh.devices.reshape(-1, Y, 4, 2, L), ("grp", "y", "a", "b", "l"))
     rows = P(("grp", *ALL))
     head = P(ALL)
     return jax.shard_map(

time: 136 us -> 133 us (0.978)
  blocking collectives: 125 us -> 122 us
    all_to_all x1, blocking collectives: 28.7 us -> 30.5 us  [local(): lax.all_to_all(spread(far, student_head, teacher_head), NEAR, 0, 0)]
    all_gather x1 -> x2, blocking collectives: 36 us -> 34.3 us  [local(): far = lax.all_gather(lax.all_gather(mine, 'a'), 'b').reshape(H, 2, ds + dt)]
where the time goes in v6:
time: 133 us
  blocking collectives  122 us (92%)
  Pallas kernels  9.21 us (7%)
  other arithmetic  1.61 us (1%)
    all_gather x2, blocking collectives, local(): far = lax.all_gather(lax.all_gather(mine, 'a'), 'b').reshape(H, 2, ds + dt)  34.3 us
    all_to_all x1, blocking collectives, local(): lax.all_to_all(spread(far, student_head, teacher_head), NEAR, 0, 0)  30.5 us
    all_to_all x1, blocking collectives, to_all(): lax.all_to_all(jnp.broadcast_to(x[None], (size, *x.shape)), axis, 0, 0)  22.7 us
    all_to_all x1, blocking collectives, local(): near_sums = lax.all_to_all(parts.reshape(Y * L, H * 2, ds), NEAR, 0, 0)  18.3 us
    all_to_all x1, blocking collectives, local(): far_sums = lax.all_to_all(fold(near_sums), FAR, 0, 0)  16.2 us
    pallas_call x1, Pallas kernels, logits(): pl.pallas_call(logits_kernel, out_shape=(jax.ShapeDtypeStruct((rows, entr...  6.6 us

profile of v6, /device:TPU:6, one launch (start us, length us, event | category | flops | bytes accessed | tf_op | source)
XLA Modules:
  0.0 133.0 jit_solution(2360059706530834958)
XLA Ops:
  0.0 0.8 maximum_bitcast_fusion
  0.8 25.9 %all-gather.2 = bf16[4,2,9216]{2,1,0:T(2,128)(2,1)S(1)} all-gather(bf16[1,2,9216]{2,1,0:T(2,128)(2,1)S(1)} %maximum_bitcast_fusion), channel_id=2, replica_groups=mesh['grp'=8,'y'=4,'a'=4,'b'=2,'l'=2] {'a'}, dimensions={0}, use_global_device_ids=true | all-gather | bytes 184320 | tf_op jit(solution)/shard_map/all_gather | solution.py:142
  26.7 0.0 slice-start
  26.7 8.4 %all-gather.1.far_ref = bf16[8,2,9216]{2,1,0:T(2,128)(2,1)S(1)} all-gather(bf16[4,2,9216]{2,1,0:T(2,128)(2,1)S(1)} %all-gather.2), channel_id=3, replica_groups=mesh['grp'=8,'y'=4,'a'=4,'b'=2,'l'=2] {'b'}, dimensions={0}, use_global_device_ids=true | all-gather | bytes 442368 | tf_op jit(solution)/shard_map/all_gather | solution.py:142
  35.1 0.0 slice-start.1
  35.1 0.0 slice-start.2
  35.1 0.0 slice-start.3
  35.1 0.0 copy-start
  35.1 0.2 shard_map.55
  35.3 30.5 %all_to_all.20 = bf16[8,16,9216]{2,1,0:T(8,128)(2,1)S(1)} all-to-all(bf16[8,16,9216]{2,1,0:T(8,128)(2,1)S(1)} %shard_map.55), channel_id=1, replica_groups=mesh['grp'=8,'y'=4,'a'=4,'b'=2,'l'=2] {'y','l'}, dimensions={0} | all-to-all | bytes 4718592 | tf_op jit(solution)/shard_map/all_to_all | solution.py:143
  65.9 0.0 slice-done
  65.9 0.0 slice-done.1
  65.9 0.0 slice-done.2
  65.9 0.0 slice-done.3
  65.9 0.0 copy-done
  65.9 6.6 %shard_map.56 = (f32[128,1280]{1,0:T(8,128)S(1)}, f32[128,1280]{1,0:T(8,128)S(1)}, f32[2,128]{1,0:T(2,128)S(1)}, f32[2,128]{1,0:T(2,128)S(1)}) custom-call(bf16[128,9216]{1,0:T(8,128)(2,1)S(1)} %bitcast.6, bf16[1280,5120]{1,0:T(8,128)(2,1)S(1)} %bitcast.5, bf16[1280,4096]{1,0:T(8,128)(2,1)S(1)} %copy-done), custom_call_target="tpu_custom_call" | custom-call | tf_op jit(solution)/shard_map/pallas_call | solution.py:92
  72.5 22.7 %all_to_all.21.all_ref = f32[64,2,128]{2,1,0:T(2,128)S(1)} all-to-all(f32[64,2,128]{2,1,0:T(2,128)S(1)} %broadcast_in_dim.2), channel_id=1, replica_groups=mesh['grp'=8,'y'=4,'a'=4,'b'=2,'l'=2] {'y','a','b','l'}, dimensions={0} | all-to-all | bytes 131072 | tf_op jit(solution)/shard_map/all_to_all | solution.py:19
  95.2 2.2 %shard_map.57 = bf16[128,5120]{1,0:T(8,128)(2,1)S(1)} custom-call(f32[128,1280]{1,0:T(8,128)S(1)} %get-tuple-element.9.student_exp, f32[128,1280]{1,0:T(8,128)S(1)} %get-tuple-element.10.teacher_exp, f32[2,128]{1,0:T(2,128)S(1)} %get-tuple-element.11.tops_ref, f32[64,2,128]{2,1,0:T(2,128)S(1)} %all_to_all.21.all_ref, bf16[1280,5120]{1,0:T(8,128)(2,1)S(1)} %bitcast.5), custom_call_target="tpu_custom_call" | custom-call | tf_op jit(solution)/shard_map/pallas_call | solution.py:129
  97.4 0.0 copy-start.1
  97.5 18.3 %all_to_all.22.sums_ref = bf16[8,16,5120]{2,1,0:T(8,128)(2,1)S(1)} all-to-all(bf16[8,16,5120]{2,1,0:T(8,128)(2,1)S(1)} %bitcast.7), channel_id=1, replica_groups=mesh['grp'=8,'y'=4,'a'=4,'b'=2,'l'=2] {'y','l'}, dimensions={0} | all-to-all | bytes 2621440 | tf_op jit(solution)/shard_map/all_to_all | solution.py:147
  115.8 0.2 shard_map.58
  116.0 16.2 %all_to_all.23 = bf16[8,2,5120]{2,1,0:T(2,128)(2,1)S(1)} all-to-all(bf16[8,2,5120]{2,1,0:T(2,128)(2,1)S(1)} %shard_map.58), channel_id=1, replica_groups=mesh['grp'=8,'y'=4,'a'=4,'b'=2,'l'=2] {'b','a'}, dimensions={0} | all-to-all | bytes 327680 | tf_op jit(solution)/shard_map/all_to_all | solution.py:148
  132.2 0.1 convert_reduce_fusion
  132.3 0.0 copy-done.1
  132.3 0.7 multiply_convert_fusion
  (2 shorter events, 0.0 us)
Async XLA Ops:
  26.7 39.2 %slice-start = ((s8[13107200]{0:T(1024)(128)(4,1)}), s8[4194304]{0:T(1024)(128)(4,1)S(1)}, s32[]{:S(2)}) async-start(s8[13107200]{0:T(1024)(128)(4,1)} %bitcast.4), calls=%async_computation.4 | async-start | bytes 8388608
  35.1 30.8 %slice-start.1 = ((s8[13107200]{0:T(1024)(128)(4,1)}), s8[4194304]{0:T(1024)(128)(4,1)S(1)}, s32[]{:S(2)}) async-start(s8[13107200]{0:T(1024)(128)(4,1)} %bitcast.4), calls=%async_computation.5 | async-start | bytes 8388608
  35.1 30.8 %slice-start.2 = ((s8[13107200]{0:T(1024)(128)(4,1)}), s8[4194304]{0:T(1024)(128)(4,1)S(1)}, s32[]{:S(2)}) async-start(s8[13107200]{0:T(1024)(128)(4,1)} %bitcast.4), calls=%async_computation.6 | async-start | bytes 8388608
  35.1 30.8 %slice-start.3 = ((s8[13107200]{0:T(1024)(128)(4,1)}), s8[524288]{0:T(1024)(128)(4,1)S(1)}, s32[]{:S(2)}) async-start(s8[13107200]{0:T(1024)(128)(4,1)} %bitcast.4), calls=%async_computation.7 | async-start | bytes 1048576
  35.1 30.8 %copy-start = (bf16[1280,4096]{1,0:T(8,128)(2,1)S(1)}, bf16[1280,4096]{1,0:T(8,128)(2,1)}, u32[]{:S(2)}) copy-start(bf16[1280,4096]{1,0:T(8,128)(2,1)} %teacher_ref.1) | copy-start | bytes 31457284
  97.4 34.9 %copy-start.1 = (f32[2]{0:T(128)S(1)}, f32[2]{0:T(128)}, u32[]{:S(2)}) copy-start(f32[2]{0:T(128)} %param.9) | copy-start | bytes 28
